TPU v7x, 128 devices: a whole 4x4x4 slice. The times are simulated.
128 devices in a mesh: zone: 4 (over z), rank: 32 (over y, x, core).
Axes of the slice: x: 4, y: 4, z: 4, core: 2. Of those that a mesh axis runs over, the one named last changes fastest.
Arguments:
- adjoint_rhs: float32 [40, 32768], P(None, ('zone', 'rank'))
- diag_blocks: float32 [40, 40, 32768], P(None, None, ('zone', 'rank'))
- precond: float32 [40, 40, 32768], P(None, None, ('zone', 'rank'))
- face_blocks: float32 [6, 40, 40, 32768], P(None, None, None, ('zone', 'rank')), may hold values from -0.625 to 0.625
- face_nbrs: int32 [6, 32768], P(None, ('zone', 'rank')), may hold values from 0 to 383, as said below
- stash_blocks: float32 [1600, 65536], P(None, ('zone', 'rank')), may hold values from -0.625 to 0.625
- stash_rows: int32 [65536], P(('zone', 'rank')), may hold values from 0 to 255
- stash_cols: int32 [65536], P(('zone', 'rank')), may hold values from 0 to 255
- stash_counts: int32 [16384], P(('zone', 'rank')), may hold values from 0 to 4, as said below
Outputs:
- adjoint: float32 [40, 32768], P(None, ('zone', 'rank'))
- residual: float32 [40, 32768], P(None, ('zone', 'rank'))
Inputs may be any that keep to these rules, and one draw needn't show every extreme that they name: `stash_counts`: some device receives 4 live slots from every device; the devices that receive this many are drawn from the seed. `face_nbrs`: every device has a face neighbour at position 0 and one at the last position.
All inputs are finite; a program needn't handle non-finite values.
Results may differ from a plain program's by a relative error of at most 0.0001.
Values sent between devices are 32-bit elements; how exact they have to be, the bound alone decides.
A program may use at most 128 MiB of HBM per device.

v0:
```python
import jax
import jax.numpy as jnp
from jax import lax
from jax.experimental import pallas as pl
from jax.experimental.pallas import tpu as pltpu
from jax.sharding import PartitionSpec as P

B = 40
TILES = B // 8
LANES = 128
ZONES, RANKS = 4, 32
DEVICES = ZONES * RANKS
CAP = 4
EPS = 1e-6
DOWN = 2.0**-40
UP = 2.0**40
MESH = pl.DeviceIdType.MESH
F32 = jnp.float32

HOPS = (0, 1, 2, 1)
PLANE = [(dy, dx, dc) for dy in range(4) for dx in range(4) for dc in range(2)]


def plane_hops(offset):
    return HOPS[offset[0]] + HOPS[offset[1]]


OTHERS = sorted(
    ((dz, offset) for dz in range(4) for offset in PLANE if dz or any(offset)),
    key=lambda other: -(HOPS[other[0]] + plane_hops(other[1])),
)
KINDS = sorted(
    ((kind, offset) for kind in (2, 1, -1, 0) for offset in PLANE if kind or any(offset)),
    key=lambda other: -(abs(other[0]) + plane_hops(other[1])),
)


def gather_lanes(tile, index):
    return jnp.take_along_axis(tile, index, axis=1)


def add_up(terms):
    terms = list(terms)
    while len(terms) > 1:
        terms = [terms[k] + terms[k + 1] if k + 1 < len(terms) else terms[k] for k in range(0, len(terms), 2)]
    return terms[0]


def total(value):
    return jnp.sum(jnp.sum(value, axis=0, keepdims=True), axis=1, keepdims=True)


def kernel(
    rhs_hbm, diag_hbm, precond_hbm, face_hbm, nbrs_hbm, stash_hbm, rows_hbm, cols_hbm, counts_hbm,
    out_ref,
    rhs, precond, blocks, stash, nbrs, rows, cols, counts,
    near, halo_out, halo_in, search0, image, sending,
    send, arrived, onehot, dots, dots_in,
    load_sem, own_sem, send_sem, recv_sem, halo_send_sem, halo_recv_sem,
):
    zone, rank = lax.axis_index("zone"), lax.axis_index("rank")
    y, x, core = rank // 8, (rank // 2) % 4, rank % 2
    me = zone * RANKS + rank
    zs = [(zone + d) % 4 for d in range(4)]
    ys = [((y + d) % 4) * 8 for d in range(4)]
    xs = [((x + d) % 4) * 2 for d in range(4)]
    cs = [(core + d) % 2 for d in range(2)]
    yxs = [[ys[a] + xs[b] for b in range(4)] for a in range(4)]

    def rank_at(offset):
        dy, dx, dc = offset
        return yxs[dy][dx] + cs[dc]

    def place(other):
        return zs[other[0]], rank_at(other[1])

    mate = 3 - 2 * (zone % 2)
    ahead = {2: 2, 1: mate, -1: 4 - mate, 0: 0}
    far_pair = ((zone + 2) % 4) // 2
    pairs = (far_pair, 1 - far_pair)
    chunks = tuple(2 * p + k for p in pairs for k in range(2))

    barrier = pltpu.get_barrier_semaphore()

    def greet(others):
        for other in others:
            pl.semaphore_signal(barrier, inc=1, device_id=place(other), device_id_type=MESH)

    greet(OTHERS)

    small = [
        pltpu.make_async_copy(rhs_hbm, rhs, load_sem.at[0]),
        pltpu.make_async_copy(rows_hbm, rows, load_sem.at[1]),
        pltpu.make_async_copy(counts_hbm, counts, load_sem.at[2]),
        pltpu.make_async_copy(cols_hbm, cols, load_sem.at[3]),
        pltpu.make_async_copy(nbrs_hbm, nbrs, load_sem.at[4]),
    ]
    load_precond = pltpu.make_async_copy(precond_hbm, precond, load_sem.at[5])
    load_stash = [
        pltpu.make_async_copy(
            stash_hbm.at[:, pl.ds(pl.multiple_of(c * LANES, LANES), LANES)], stash.at[c], load_sem.at[6 + k]
        )
        for k, c in enumerate(chunks)
    ]
    load_diag = pltpu.make_async_copy(diag_hbm, blocks.at[0], load_sem.at[10])
    load_face = pltpu.make_async_copy(face_hbm, blocks.at[pl.ds(1, 6)], load_sem.at[11])
    for load in [*small, load_precond, *load_stash, load_diag, load_face]:
        load.start()

    lane = lax.broadcasted_iota(jnp.int32, (8, LANES), 1)
    sub = lax.broadcasted_iota(jnp.int32, (8, LANES), 0)
    left = lane < LANES // 2
    pair = 2 * (lane % (LANES // 2))

    def halos(step):
        return (
            pltpu.make_async_remote_copy(
                src_ref=halo_out.at[step, 1], dst_ref=halo_in.at[step, 0],
                send_sem=halo_send_sem.at[step, 0], recv_sem=halo_recv_sem.at[step, 0],
                device_id=(zone, rank + 1), device_id_type=MESH,
            ),
            pltpu.make_async_remote_copy(
                src_ref=halo_out.at[step, 0], dst_ref=halo_in.at[step, 1],
                send_sem=halo_send_sem.at[step, 1], recv_sem=halo_recv_sem.at[step, 1],
                device_id=(zone, rank - 1), device_id_type=MESH,
            ),
        )

    def start_halos(step):
        up, down = halos(step)

        @pl.when(rank < RANKS - 1)
        def _():
            up.start()

        @pl.when(rank > 0)
        def _():
            down.start()

    def wait_halos(step):
        up, down = halos(step)

        @pl.when(rank > 0)
        def _():
            up.wait_recv()

        @pl.when(rank == 0)
        def _():
            halo_in[step, 0] = jnp.zeros((B, LANES), F32)

        @pl.when(rank < RANKS - 1)
        def _():
            down.wait_recv()

        @pl.when(rank == RANKS - 1)
        def _():
            halo_in[step, 1] = jnp.zeros((B, LANES), F32)

        @pl.when(rank < RANKS - 1)
        def _():
            up.wait_send()

        @pl.when(rank > 0)
        def _():
            down.wait_send()

    def rows_from(tiles):
        tiles = [
            jnp.where(sub < 4, one, two) + pltpu.roll(jnp.where(sub < 4, two, one), 4, 0)
            for one, two in zip(tiles[:4], tiles[4:])
        ]
        for shift in (2, 1):
            half = len(tiles) // 2
            tiles = [
                jnp.where(sub % (2 * shift) < shift, one + pltpu.roll(one, 8 - shift, 0), two + pltpu.roll(two, shift, 0))
                for one, two in zip(tiles[:half], tiles[half:])
            ]
        return tiles[0]

    def apply_precond(step):
        def rows_of(block, _):
            first = pl.multiple_of(block * 8, 8)
            for c in range(2):
                half = slice(c * LANES, c * LANES + LANES)
                vector = [near[0, t * 8 : t * 8 + 8, half] for t in range(TILES)]
                halo_out[step, c, pl.ds(first, 8), :] = rows_from([
                    add_up(precond[first + i, t * 8 : t * 8 + 8, half] * vector[t] for t in range(TILES)) for i in range(8)
                ])
            return 0

        lax.fori_loop(0, TILES, rows_of, 0, unroll=TILES)

    def expand_counts(c):
        tile = jnp.broadcast_to(counts[...], (8, LANES))
        return gather_lanes(tile, c * 32 + lane // CAP)

    def gather_sending(step, c):
        at = jnp.broadcast_to(rows[pl.ds(c, 1), :], (8, LANES))
        live = jnp.where(lane % CAP < expand_counts(c), 1.0, 0.0)
        low, at = at < LANES, at % LANES
        for t in range(TILES):
            first = gather_lanes(halo_out[step, 0, t * 8 : t * 8 + 8, :], at)
            second = gather_lanes(halo_out[step, 1, t * 8 : t * 8 + 8, :], at)
            sending[c, t * 8 : t * 8 + 8, :] = jnp.where(low, first, second) * live

    def couple(pair_of):
        def step_of(i, acc):
            row = pl.multiple_of(i * B, 8)
            added = []
            for c in pair_of:
                factor = jnp.broadcast_to(sending[c, pl.ds(i, 1), :], (8, LANES))
                added += [stash[c, pl.ds(row + t * 8, 8), :] * factor for t in range(TILES)]
            return tuple(old + new for old, new in zip(acc, added))

        zero = jnp.zeros((8, LANES), F32)
        sums = lax.fori_loop(0, B, step_of, (zero,) * (2 * TILES), unroll=B)
        return sums[:TILES], sums[TILES:]

    def pack(step, p, couplings, scalars):
        zero = jnp.zeros((8, LANES), F32)
        tiles = []
        for h in range(2):
            for t in range(TILES):
                first = gather_lanes(couplings[0][t], pair + h)
                second = gather_lanes(couplings[1][t], pair + h)
                tiles.append(jnp.where(left, first, second))
            first = gather_lanes(jnp.broadcast_to(cols[pl.ds(2 * p, 1), :], (8, LANES)), pair + h)
            second = gather_lanes(jnp.broadcast_to(cols[pl.ds(2 * p + 1, 1), :], (8, LANES)), pair + h)
            extra = jnp.where(sub == 0, jnp.where(left, first, second).astype(F32), 0.0)
            for place_of, scalar in enumerate(scalars):
                extra = jnp.where(sub == 1 + place_of, scalar, extra)
            tiles += [extra, zero, zero]
        turned = jnp.concatenate(tiles, axis=0).T
        for d in range(64):
            send[step, 64 * p + d] = turned[2 * d : 2 * d + 2, :]

    def message(step, kind, offset):
        z, r = (zone + ahead[kind]) % 4, rank_at(offset)
        spot = offset[0] * 8 + offset[1] * 2 + offset[2]
        return pltpu.make_async_remote_copy(
            src_ref=send.at[step, z * RANKS + r], dst_ref=arrived.at[step, ahead[kind] * RANKS + spot],
            send_sem=send_sem.at[step], recv_sem=recv_sem.at[step],
            device_id=(z, r), device_id_type=MESH,
        )

    def own(step):
        return pltpu.make_async_copy(send.at[step, me], arrived.at[step, 0], own_sem.at[step])

    def all_arrived(step):
        others = arrived.at[step, pl.ds(1, DEVICES - 1)]
        pltpu.make_async_copy(others, others, recv_sem.at[step]).wait()
        own(step).wait()

    def prepare(step, k, scalars):
        pair_of = chunks[2 * k : 2 * k + 2]
        for j, c in enumerate(pair_of):
            if step == 0:
                load_stash[2 * k + j].wait()
            gather_sending(step, c)
        pack(step, pairs[k], couple(pair_of), scalars)

    def first_out(other):
        return other[0] > 0

    def post(step, first):
        for other in KINDS:
            if first_out(other) == first:
                message(step, *other).start()

    def apply_local(step):
        for t in range(TILES):
            tile = slice(t * 8, t * 8 + 8)
            zero_tile = halo_out[step, 0, tile, :]
            one_tile = halo_out[step, 1, tile, :]
            rim_tile = jnp.where(left, halo_in[step, 1, tile, :], halo_in[step, 0, tile, :])
            near[0, tile, :LANES] = zero_tile
            near[0, tile, LANES:] = one_tile
            for f in range(6):
                for c in range(2):
                    at = jnp.broadcast_to(nbrs[f : f + 1, c * LANES : c * LANES + LANES], (8, LANES))
                    index = (at + 64) % LANES
                    found = jnp.where(
                        (at >= 64) & (at < 192), gather_lanes(zero_tile, index),
                        jnp.where((at >= 192) & (at < 320), gather_lanes(one_tile, index), gather_lanes(rim_tile, index)),
                    )
                    near[1 + f, tile, c * LANES : c * LANES + LANES] = found
        if step == 0:
            load_diag.wait()
            load_face.wait()

        def rows_of(block, _):
            first = pl.multiple_of(block * 8, 8)
            for c in range(2):
                half = slice(c * LANES, c * LANES + LANES)
                sums = [None] * 8
                for b in range(7):
                    vector = [near[b, t * 8 : t * 8 + 8, half] for t in range(TILES)]
                    for i in range(8):
                        term = add_up(blocks[b, first + i, t * 8 : t * 8 + 8, half] * vector[t] for t in range(TILES))
                        sums[i] = term if b == 0 else sums[i] + term
                image[pl.ds(first, 8), half] = rows_from(sums)
            return 0

        lax.fori_loop(0, TILES, rows_of, 0)

    def received(step):
        return jnp.concatenate([arrived[step, k] for k in range(DEVICES)], axis=0)

    def sums_of(table):
        tile = add_up(table[8 * k : 8 * k + 8, :] for k in range(2 * DEVICES // 8))
        return jnp.sum(tile, axis=0, keepdims=True) * 0.5

    def scattered(table):
        turned = table.T
        halves = []
        for h in range(2):
            rest = turned[64 * h : 64 * h + 48, :]
            parts = []
            for _ in range(3):
                part = rest.astype(jnp.bfloat16)
                parts.append(part)
                rest = rest - part.astype(F32)
            halves.append(jnp.concatenate(parts, axis=0))
        product = jnp.dot(jnp.concatenate(halves, axis=1), onehot[...], preferred_element_type=F32)
        return product[:B] + product[48 : 48 + B] + product[96 : 96 + B]

    small[0].wait()
    near[0] = rhs[...] * DOWN
    square = total(rhs[...] * rhs[...])
    load_precond.wait()
    apply_precond(0)
    small[1].wait()
    small[2].wait()
    small[3].wait()
    small[4].wait()
    for k in range(2):
        prepare(0, k, (square,))
    pl.semaphore_wait(barrier, DEVICES - 1)
    post(0, True)
    start_halos(0)
    post(0, False)
    own(0).start()
    wait_halos(0)
    apply_local(0)
    all_arrived(0)
    table = received(0)
    element = lax.broadcasted_iota(jnp.int32, (256, 256), 1).astype(F32)
    for h in range(2):
        column = table[:, 64 * h + B : 64 * h + B + 1]
        onehot[256 * h : 256 * h + 256, :] = jnp.where(element == column, 1.0, 0.0).astype(jnp.bfloat16)
    sums = sums_of(table)
    square = sums[:, B + 1 : B + 2]
    beta = jnp.sqrt(square + EPS)
    shrunk = 1.0 / beta
    basis0 = rhs[...] * shrunk
    factor = UP * shrunk
    work0 = (image[...] + scattered(table)) * factor
    search0[:, :LANES] = halo_out[0, 0] * factor
    search0[:, LANES:] = halo_out[0, 1] * factor

    near[0] = work0
    apply_precond(1)
    scalars = (total(work0 * basis0), total(work0 * work0))
    prepare(1, 0, scalars)
    post(1, True)
    start_halos(1)
    prepare(1, 1, scalars)
    post(1, False)
    own(1).start()
    wait_halos(1)
    apply_local(1)
    all_arrived(1)
    table = received(1)
    sums = sums_of(table)
    h00 = sums[:, B + 1 : B + 2]
    shrink = 1.0 / jnp.sqrt(sums[:, B + 2 : B + 3] + EPS)
    unit = square / (square + EPS)
    work1 = work0 - h00 * basis0
    second = (image[...] + scattered(table) - h00 * work0) * shrink

    values = (
        total(work1 * work1), total(work1 * basis0), total(second * basis0), total(second * work1), total(second * second)
    )
    row_lane = lax.broadcasted_iota(jnp.int32, (1, LANES), 1)
    mine = jnp.zeros((1, LANES), F32)
    for place_of, value in enumerate(values):
        mine = jnp.where(row_lane == place_of, value, mine)
    dots[...] = mine
    dots_in[0] = mine

    def tell(other):
        dz, (dy, dx, dc) = other
        return pltpu.make_async_remote_copy(
            src_ref=dots, dst_ref=dots_in.at[dz * RANKS + dy * 8 + dx * 2 + dc],
            send_sem=send_sem.at[2], recv_sem=recv_sem.at[2],
            device_id=place(other), device_id_type=MESH,
        )

    for other in OTHERS:
        tell(other).start()
    others = dots_in.at[pl.ds(1, DEVICES - 1)]
    pltpu.make_async_copy(others, others, recv_sem.at[2]).wait()
    sums = add_up(dots_in[k] for k in range(DEVICES))
    n1, cross, a, b, d = (sums[:, k : k + 1] for k in range(5))
    n1_eps = n1 + EPS
    across = b - a * cross
    along = across / n1_eps
    left_over = d - 2.0 * a * a + unit * a * a - 2.0 * along * b + along * along * n1 + 2.0 * a * along * cross
    n00 = h00 * h00 + n1_eps
    mixed = h00 * a + across
    lower = mixed / n00
    corner = a * a + along * across + (jnp.maximum(left_over, 0.0) + EPS * n1_eps * shrink * shrink)
    y1 = beta * (a - lower * h00) / (corner - lower * mixed)
    c0 = (beta * h00 - mixed * y1) / n00
    y1_small = y1 * shrink
    own_part = c0 - y1_small * h00
    for c in range(2):
        half = slice(c * LANES, c * LANES + LANES)
        out_ref[0, :, half] = own_part * search0[:, half] + y1_small * halo_out[1, c]
    out_ref[1] = rhs[...] - c0 * work0 - y1 * second

    for step in range(2):
        others = arrived.at[step, pl.ds(1, DEVICES - 1)]
        pltpu.make_async_copy(others, others, send_sem.at[step]).wait()
    others = dots_in.at[pl.ds(1, DEVICES - 1)]
    pltpu.make_async_copy(others, others, send_sem.at[2]).wait()


def per_device(rhs, diag, precond, face, nbrs, stash, rows, cols, counts):
    arrays = (
        rhs, diag, precond, face, nbrs, stash, rows.reshape(4, LANES), cols.reshape(4, LANES), counts.reshape(1, LANES)
    )
    anywhere = pl.BlockSpec(memory_space=pl.ANY)
    out = pl.pallas_call(
        kernel,
        out_shape=jax.ShapeDtypeStruct((2, B, 256), F32),
        in_specs=[anywhere] * 9,
        out_specs=pl.BlockSpec(memory_space=pltpu.VMEM),
        scratch_shapes=[
            pltpu.VMEM((B, 256), F32),
            pltpu.VMEM((B, B, 256), F32),
            pltpu.VMEM((7, B, B, 256), F32),
            pltpu.VMEM((4, B * B, LANES), F32),
            pltpu.VMEM((6, 256), jnp.int32),
            pltpu.VMEM((4, LANES), jnp.int32),
            pltpu.VMEM((4, LANES), jnp.int32),
            pltpu.VMEM((1, LANES), jnp.int32),
            pltpu.VMEM((7, B, 256), F32),
            pltpu.VMEM((2, 2, B, LANES), F32),
            pltpu.VMEM((2, 2, B, LANES), F32),
            pltpu.VMEM((B, 256), F32),
            pltpu.VMEM((B, 256), F32),
            pltpu.VMEM((4, B, LANES), F32),
            pltpu.VMEM((2, DEVICES, 2, LANES), F32),
            pltpu.VMEM((2, DEVICES, 2, LANES), F32),
            pltpu.VMEM((512, 256), jnp.bfloat16),
            pltpu.VMEM((1, LANES), F32),
            pltpu.VMEM((DEVICES, 1, LANES), F32),
            pltpu.SemaphoreType.DMA((12,)),
            pltpu.SemaphoreType.DMA((2,)),
            pltpu.SemaphoreType.DMA((3,)),
            pltpu.SemaphoreType.DMA((3,)),
            pltpu.SemaphoreType.DMA((2, 2)),
            pltpu.SemaphoreType.DMA((2, 2)),
        ],
        compiler_params=pltpu.CompilerParams(
            collective_id=0, has_side_effects=True, vmem_limit_bytes=48 * 2**20
        ),
        name="gmres",
    )(*(pltpu.with_memory_space_constraint(array, pltpu.HBM) for array in arrays))
    return out[0], out[1]


def solution(mesh):
    spread = ("zone", "rank")
    return jax.shard_map(
        per_device,
        mesh=mesh,
        in_specs=(
            P(None, spread),
            P(None, None, spread),
            P(None, None, spread),
            P(None, None, None, spread),
            P(None, spread),
            P(None, spread),
            P(spread),
            P(spread),
            P(spread),
        ),
        out_specs=(P(None, spread), P(None, spread)),
        check_vma=False,
    )
```

profile of v0, /device:TPU:1, one launch (start us, length us, event | category | flops | bytes accessed | tf_op | source)
XLA Modules:
  0.0 30.3 jit_solution(12341300393016357818)
XLA Ops:
  0.6 29.0 %gmres.1 = f32[2,40,256]{2,1,0:T(8,128)S(1)} custom-call(f32[40,256]{1,0:T(8,128)} %rhs_hbm.1, f32[40,40,256]{2,1,0:T(8,128)} %diag_hbm.1, f32[40,40,256]{2,1,0:T(8,128)} %precond_hbm.1, f32[6,40,40,256]{3,2,1,0:T(8,128)} %face_hbm.1, s32[6,256]{1,0:T(8,128)} %nbrs_hbm.1, f32[1600,512]{1,0:T(8,128)} %stash_hbm.1, s32[4,128]{1,0:T(4,128)} %bitcast.7, ...), custom_call_target="tpu_custom_call" | custom-call | tf_op jit(solution)/shard_map/gmres/pallas_call | solution.py:434
  29.6 0.6 %slice_bitcast_fusion = (f32[40,256]{1,0:T(8,128)}, f32[40,256]{1,0:T(8,128)}) fusion(f32[2,40,256]{2,1,0:T(8,128)S(1)} %gmres.1), kind=kLoop, calls=%fused_computation | loop fusion | bytes 163840 | tf_op jit(solution)/shard_map/squeeze | solution.py:471
where the time goes:
time: 30.4 us; the launch traced here: 30.3 us
  Pallas kernels  29 us (95%)
  local copies, waits for them, and re-layouts  0.64 us (2%)
  between operations  0.64 us (2%)
    pallas_call x1, Pallas kernels, per_device(): pl.pallas_call(kernel, out_shape=jax.ShapeDtypeStruct((2, B, 256), F32),...  29 us
    squeeze x1, local copies, waits for them, and re-layouts, per_device(): return (out[0], out[1])  0.64 us

commit v1 on v0

--- a/solution.py
+++ b/solution.py
@@ -7,6 +7,7 @@
 
 B = 40
 TILES = B // 8
+RIM_TILES = (TILES + 1) // 2
 LANES = 128
 ZONES, RANKS = 4, 32
 DEVICES = ZONES * RANKS
@@ -39,6 +40,10 @@
     return jnp.take_along_axis(tile, index, axis=1)
 
 
+def half_turn(tile):
+    return pltpu.roll(tile, LANES // 2, 1)
+
+
 def add_up(terms):
     terms = list(terms)
     while len(terms) > 1:
@@ -54,7 +59,7 @@
     rhs_hbm, diag_hbm, precond_hbm, face_hbm, nbrs_hbm, stash_hbm, rows_hbm, cols_hbm, counts_hbm,
     out_ref,
     rhs, precond, blocks, stash, nbrs, rows, cols, counts,
-    near, halo_out, halo_in, search0, image, sending,
+    near, search, rim_out, rim_in, search0, image, sending,
     send, arrived, onehot, dots, dots_in,
     load_sem, own_sem, send_sem, recv_sem, halo_send_sem, halo_recv_sem,
 ):
@@ -115,12 +120,12 @@
     def halos(step):
         return (
             pltpu.make_async_remote_copy(
-                src_ref=halo_out.at[step, 1], dst_ref=halo_in.at[step, 0],
+                src_ref=rim_out.at[step, 0], dst_ref=rim_in.at[step, 0],
                 send_sem=halo_send_sem.at[step, 0], recv_sem=halo_recv_sem.at[step, 0],
                 device_id=(zone, rank + 1), device_id_type=MESH,
             ),
             pltpu.make_async_remote_copy(
-                src_ref=halo_out.at[step, 0], dst_ref=halo_in.at[step, 1],
+                src_ref=rim_out.at[step, 1], dst_ref=rim_in.at[step, 1],
                 send_sem=halo_send_sem.at[step, 1], recv_sem=halo_recv_sem.at[step, 1],
                 device_id=(zone, rank - 1), device_id_type=MESH,
             ),
@@ -128,6 +133,15 @@
 
     def start_halos(step):
         up, down = halos(step)
+        for k in range(RIM_TILES):
+            near_rows = slice(8 * k, 8 * k + 8)
+            last, first = search[step, 1, near_rows, :], search[step, 0, near_rows, :]
+            if RIM_TILES + k < TILES:
+                far_rows = slice(8 * (RIM_TILES + k), 8 * (RIM_TILES + k) + 8)
+                last = jnp.where(left, half_turn(search[step, 1, far_rows, :]), last)
+                first = jnp.where(left, first, half_turn(search[step, 0, far_rows, :]))
+            rim_out[step, 0, near_rows, :] = last
+            rim_out[step, 1, near_rows, :] = first
 
         @pl.when(rank < RANKS - 1)
         def _():
@@ -146,7 +160,7 @@
 
         @pl.when(rank == 0)
         def _():
-            halo_in[step, 0] = jnp.zeros((B, LANES), F32)
+            rim_in[step, 0] = jnp.zeros((8 * RIM_TILES, LANES), F32)
 
         @pl.when(rank < RANKS - 1)
         def _():
@@ -154,7 +168,7 @@
 
         @pl.when(rank == RANKS - 1)
         def _():
-            halo_in[step, 1] = jnp.zeros((B, LANES), F32)
+            rim_in[step, 1] = jnp.zeros((8 * RIM_TILES, LANES), F32)
 
         @pl.when(rank < RANKS - 1)
         def _():
@@ -183,7 +197,7 @@
             for c in range(2):
                 half = slice(c * LANES, c * LANES + LANES)
                 vector = [near[0, t * 8 : t * 8 + 8, half] for t in range(TILES)]
-                halo_out[step, c, pl.ds(first, 8), :] = rows_from([
+                search[step, c, pl.ds(first, 8), :] = rows_from([
                     add_up(precond[first + i, t * 8 : t * 8 + 8, half] * vector[t] for t in range(TILES)) for i in range(8)
                 ])
             return 0
@@ -199,8 +213,8 @@
         live = jnp.where(lane % CAP < expand_counts(c), 1.0, 0.0)
         low, at = at < LANES, at % LANES
         for t in range(TILES):
-            first = gather_lanes(halo_out[step, 0, t * 8 : t * 8 + 8, :], at)
-            second = gather_lanes(halo_out[step, 1, t * 8 : t * 8 + 8, :], at)
+            first = gather_lanes(search[step, 0, t * 8 : t * 8 + 8, :], at)
+            second = gather_lanes(search[step, 1, t * 8 : t * 8 + 8, :], at)
             sending[c, t * 8 : t * 8 + 8, :] = jnp.where(low, first, second) * live
 
     def couple(pair_of):
@@ -270,9 +284,13 @@
     def apply_local(step):
         for t in range(TILES):
             tile = slice(t * 8, t * 8 + 8)
-            zero_tile = halo_out[step, 0, tile, :]
-            one_tile = halo_out[step, 1, tile, :]
-            rim_tile = jnp.where(left, halo_in[step, 1, tile, :], halo_in[step, 0, tile, :])
+            zero_tile = search[step, 0, tile, :]
+            one_tile = search[step, 1, tile, :]
+            if t < RIM_TILES:
+                rim_tile = jnp.where(left, rim_in[step, 1, tile, :], rim_in[step, 0, tile, :])
+            else:
+                packed = slice((t - RIM_TILES) * 8, (t - RIM_TILES) * 8 + 8)
+                rim_tile = half_turn(jnp.where(left, rim_in[step, 0, packed, :], rim_in[step, 1, packed, :]))
             near[0, tile, :LANES] = zero_tile
             near[0, tile, LANES:] = one_tile
             for f in range(6):
@@ -355,8 +373,8 @@
     basis0 = rhs[...] * shrunk
     factor = UP * shrunk
     work0 = (image[...] + scattered(table)) * factor
-    search0[:, :LANES] = halo_out[0, 0] * factor
-    search0[:, LANES:] = halo_out[0, 1] * factor
+    search0[:, :LANES] = search[0, 0] * factor
+    search0[:, LANES:] = search[0, 1] * factor
 
     near[0] = work0
     apply_precond(1)
@@ -416,7 +434,7 @@
     own_part = c0 - y1_small * h00
     for c in range(2):
         half = slice(c * LANES, c * LANES + LANES)
-        out_ref[0, :, half] = own_part * search0[:, half] + y1_small * halo_out[1, c]
+        out_ref[0, :, half] = own_part * search0[:, half] + y1_small * search[1, c]
     out_ref[1] = rhs[...] - c0 * work0 - y1 * second
 
     for step in range(2):
@@ -447,7 +465,8 @@
             pltpu.VMEM((1, LANES), jnp.int32),
             pltpu.VMEM((7, B, 256), F32),
             pltpu.VMEM((2, 2, B, LANES), F32),
-            pltpu.VMEM((2, 2, B, LANES), F32),
+            pltpu.VMEM((2, 2, 8 * RIM_TILES, LANES), F32),
+            pltpu.VMEM((2, 2, 8 * RIM_TILES, LANES), F32),
             pltpu.VMEM((B, 256), F32),
             pltpu.VMEM((B, 256), F32),
             pltpu.VMEM((4, B, LANES), F32),

time: 30.4 us -> 30.3 us (level)
  no operation moved by 1% of the time
where the time goes in v1:
time: 30.3 us; the launch traced here: 30.2 us
  Pallas kernels  28.9 us (95%)
  local copies, waits for them, and re-layouts  0.64 us (2%)
  between operations  0.64 us (2%)
    pallas_call x1, Pallas kernels, per_device(): pl.pallas_call(kernel, out_shape=jax.ShapeDtypeStruct((2, B, 256), F32),...  28.9 us
    squeeze x1, local copies, waits for them, and re-layouts, per_device(): return (out[0], out[1])  0.64 us

profile of v1, /device:TPU:1, one launch (start us, length us, event | category | flops | bytes accessed | tf_op | source)
XLA Modules:
  0.0 30.2 jit_solution(2144104245685480501)
XLA Ops:
  0.6 28.9 %gmres.1 = f32[2,40,256]{2,1,0:T(8,128)S(1)} custom-call(f32[40,256]{1,0:T(8,128)} %rhs_hbm.1, f32[40,40,256]{2,1,0:T(8,128)} %diag_hbm.1, f32[40,40,256]{2,1,0:T(8,128)} %precond_hbm.1, f32[6,40,40,256]{3,2,1,0:T(8,128)} %face_hbm.1, s32[6,256]{1,0:T(8,128)} %nbrs_hbm.1, f32[1600,512]{1,0:T(8,128)} %stash_hbm.1, s32[4,128]{1,0:T(4,128)} %bitcast.7, ...), custom_call_target="tpu_custom_call" | custom-call | tf_op jit(solution)/shard_map/gmres/pallas_call | solution.py:452
  29.6 0.6 %slice_bitcast_fusion = (f32[40,256]{1,0:T(8,128)}, f32[40,256]{1,0:T(8,128)}) fusion(f32[2,40,256]{2,1,0:T(8,128)S(1)} %gmres.1), kind=kLoop, calls=%fused_computation | loop fusion | bytes 163840 | tf_op jit(solution)/shard_map/squeeze | solution.py:490
